TPU v7x, 256 devices: a whole 4x4x8 slice. The times are simulated.
256 devices in a mesh: rep: 32 (over z_hi, x, core), fsdp: 8 (over y, z_lo).
Axes of the slice: x: 4, y: 4, z: 8 (z_hi: 4, z_lo: 2; z = z_hi * 2 + z_lo), core: 2. Of those that a mesh axis runs over, the one named last changes fastest.
Arguments:
- local_weights: bfloat16 [32, 5120, 512], P('rep', 'fsdp'), may hold values from -6 to 6
- global_weights: float32 [5120, 512], P('fsdp'), may hold values from -6 to 6
- momentum: float32 [5120, 512], P('fsdp'), may hold values from -6 to 6
- tokens: bfloat16 [131072, 5120], P(('rep', 'fsdp')), may hold values from -0.375 to 0.375
- key_grad: bfloat16 [131072, 512], P(('rep', 'fsdp')), may hold values from -6 to 6
Outputs:
- new_global: float32 [5120, 512], P('fsdp')
- new_momentum: float32 [5120, 512], P('fsdp')
- inner_keys: bfloat16 [131072, 512], P(('rep', 'fsdp'))
- weight_grad: bfloat16 [32, 5120, 512], P('rep', 'fsdp')
All inputs are finite; a program needn't handle non-finite values.
Results may differ from a plain program's by a relative error of at most 0.0049.
Values may be sent and summed in bfloat16 or wider, within the bound.
No kernel may reach another device: no remote copies, remote signals or barrier semaphores. Data moves between devices by JAX's collectives and lax.ppermute only.
A program may use at most 128 MiB of HBM per device.

v0:
```python
import jax
import jax.numpy as jnp
from jax import lax
from jax.sharding import PartitionSpec as P

momentum_rate = 0.9
outer_rate = 0.7


def per_device(local_weights, global_weights, momentum, tokens, key_grad):
    replicas = lax.axis_size("rep")
    outer_grad = global_weights - local_weights[0].astype(jnp.float32)
    summed = lax.psum(outer_grad, "rep")
    average = summed / replicas
    new_momentum = momentum_rate * momentum + average
    new_global = global_weights - outer_rate * (average + momentum_rate * new_momentum)
    start_weights = new_global.astype(jnp.bfloat16)
    columns = tokens
    inner_keys = jnp.dot(
        columns,
        lax.all_gather(start_weights, "fsdp", axis=0, tiled=True),
        preferred_element_type=jnp.float32,
    ).astype(jnp.bfloat16)
    columns = tokens
    grad_rows = lax.psum_scatter(
        lax.dot_general(
            columns, key_grad, (((0,), (0,)), ((), ())), preferred_element_type=jnp.float32
        ),
        "fsdp",
        scatter_dimension=0,
        tiled=True,
    )
    weight_grad = grad_rows.astype(jnp.bfloat16)[None]
    return (new_global, new_momentum, inner_keys, weight_grad)


def solution(mesh):
    placed = (
        P("rep", "fsdp", None),
        P("fsdp", None),
        P("fsdp", None),
        P(("rep", "fsdp"), None),
        P(("rep", "fsdp"), None),
    )
    return jax.shard_map(
        per_device,
        mesh=mesh,
        in_specs=placed,
        out_specs=(
            P("fsdp", None),
            P("fsdp", None),
            P(("rep", "fsdp"), None),
            P("rep", "fsdp", None),
        ),
        check_vma=False,
    )
```

profile of v0, /device:TPU:1, one launch (start us, length us, event | category | flops | bytes accessed | tf_op | source)
XLA Modules:
  0.0 642.0 jit_solution(12402348356338065704)
XLA Ops:
  7.2 0.0 copy-start
  7.2 0.0 all-reduce.2.cloned.1.call-start
  7.2 0.0 copy-start.2
  7.2 2.9 convert_subtract_fusion
  10.1 0.0 copy-start.1
  10.1 0.0 all-reduce.2.cloned.1.call-update
  10.1 0.0 all-gather.2.cloned.1.call-start
  10.2 293.2 %all-reduce.2.cloned.1.call-done = f32[640,512]{1,0:T(8,128)} async-done(((f32[640,512]{1,0:T(8,128)}), f32[640,512]{1,0:T(8,128)}) %all-reduce.2.cloned.1.call-update) | async-done | bytes 1310736 | tf_op jit(solution)/shard_map/psum | solution.py:13
  303.4 0.0 copy-done.2
  303.4 0.0 copy-done.1
  303.4 3.5 fusion.1
  306.9 0.0 all-gather.2.cloned.1.call-update
  306.9 0.0 reduce-scatter.2.cloned.1.call-start
  307.0 0.0 copy-done
  307.0 8.2 %fusion.2 = f32[5120,512]{1,0:T(8,128)} fusion(bf16[512,5120]{1,0:T(8,128)(2,1)} %param.8, bf16[512,512]{1,0:T(8,128)(2,1)S(1)} %copy-done), kind=kOutput, calls=%fused_computation.7 | convolution fusion | flops 2684354560 | bytes 16252928 | tf_op jit(solution)/shard_map/dot_general | solution.py:26
  315.2 0.0 reduce-scatter.2.cloned.1.call-update
  315.2 103.5 %all-gather.2.cloned.1.call-done = bf16[5120,512]{1,0:T(8,128)(2,1)} async-done(((bf16[640,512]{1,0:T(8,128)(2,1)}), bf16[5120,512]{1,0:T(8,128)(2,1)}) %all-gather.2.cloned.1.call-update) | async-done | bytes 5242896 | tf_op jit(solution)/shard_map/all_gather | solution.py:21
  418.7 7.0 %fusion = bf16[512,512]{0,1:T(8,128)(2,1)S(1)} fusion(bf16[5120,512]{1,0:T(8,128)(2,1)} %all-gather.2.cloned.1.call-done, bf16[512,5120]{1,0:T(8,128)(2,1)} %param.8), kind=kOutput, calls=%fused_computation.4 | convolution fusion | flops 2684616704 | bytes 11010048 | tf_op jit(solution)/shard_map/dot_general | solution.py:19
  425.7 1.0 copy.9
  426.7 206.6 %reduce-scatter.2.cloned.1.call-done = f32[640,512]{1,0:T(8,128)} async-done(((f32[5120,512]{1,0:T(8,128)}), f32[640,512]{1,0:T(8,128)}) %reduce-scatter.2.cloned.1.call-update) | async-done | bytes 1310736 | tf_op jit(solution)/shard_map/reduce_scatter | solution.py:25
  633.3 2.2 convert_bitcast_fusion
Async XLA Ops:
  7.2 299.8 %copy-start = (bf16[512,512]{1,0:T(8,128)(2,1)S(1)}, bf16[512,512]{1,0:T(8,128)(2,1)}, u32[]{:S(2)}) copy-start(bf16[512,512]{1,0:T(8,128)(2,1)} %param.9) | copy-start | bytes 1572868
  7.2 296.2 %all-reduce.2.cloned.1.call-start = ((), (), s32[]{:S(2)}) async-start(), calls=%async_computation.1 | async-start | bytes 2621440 | tf_op jit(solution)/shard_map/psum | solution.py:13
  7.2 296.1 %copy-start.2 = (f32[640,512]{1,0:T(8,128)S(1)}, f32[640,512]{1,0:T(8,128)}, u32[]{:S(2)}) copy-start(f32[640,512]{1,0:T(8,128)} %param.7) | copy-start | bytes 3932164
  10.1 293.3 %copy-start.1 = (f32[640,512]{1,0:T(8,128)S(1)}, f32[640,512]{1,0:T(8,128)}, u32[]{:S(2)}) copy-start(f32[640,512]{1,0:T(8,128)} %param.6) | copy-start | bytes 3932164
  10.1 408.6 %all-gather.2.cloned.1.call-start = ((), (), s32[]{:S(2)}) async-start(), calls=%async_computation.2 | async-start | bytes 5898240 | tf_op jit(solution)/shard_map/all_gather | solution.py:21
  306.9 326.3 %reduce-scatter.2.cloned.1.call-start = ((), (), s32[]{:S(2)}) async-start(), calls=%async_computation.3 | async-start | bytes 11796480 | tf_op jit(solution)/shard_map/reduce_scatter | solution.py:25
Sparse Core Ops, SparseCore 0:
  11.2 292.1 all-reduce.1
  307.1 111.5 all-gather.1
  421.4 211.8 reduce-scatter.1
where the time goes:
time: 642 us
  waiting for transfers between devices  603 us (94%)
  matrix products  15.1 us (2%)
  between operations  13.8 us (2%)
  other arithmetic  8.64 us (1%)
    psum x1, waiting for transfers between devices, per_device(): summed = lax.psum(outer_grad, 'rep')  293 us
    reduce_scatter x1, waiting for transfers between devices, per_device(): lax.psum_scatter(lax.dot_general(columns, key_grad, (((0,), (0,)), ((), (...  207 us
    all_gather x1, waiting for transfers between devices, per_device(): lax.all_gather(start_weights, 'fsdp', axis=0, tiled=True)  103 us
  transfers between devices with their start and end apart: 3, of which 3 were waited for; matrix products, arithmetic and copies ran while one was open for 3% of the time, Pallas kernels for 0%

commit v1 on v0

--- a/solution.py
+++ b/solution.py
@@ -18,7 +18,9 @@
     columns = tokens
     inner_keys = jnp.dot(
         columns,
-        lax.all_gather(start_weights, "fsdp", axis=0, tiled=True),
+        jnp.concatenate(
+            lax.all_to_all(jnp.stack([start_weights] * lax.axis_size("fsdp")), "fsdp", 0, 0), axis=0
+        ),
         preferred_element_type=jnp.float32,
     ).astype(jnp.bfloat16)
     columns = tokens

time: 642 us -> 549 us (0.86)
  waiting for transfers between devices: 603 us -> 448 us
  blocking collectives: 0 us -> 63.6 us
    reduce_scatter x1, waiting for transfers between devices: 207 us -> 0.01 us  [per_device(): lax.psum_scatter(lax.dot_general(columns, key_grad, (((0,), (0,)), ((), (...]
    psum x1, waiting for transfers between devices: 293 us -> 448 us  [per_device(): summed = lax.psum(outer_grad, 'rep')]
    all_gather x1 -> x0, waiting for transfers between devices: 103 us -> none  [per_device(): lax.all_gather(start_weights, 'fsdp', axis=0, tiled=True)]
    all_to_all x0 -> x1, blocking collectives: none -> 63.6 us  [per_device(): lax.all_to_all(jnp.stack([start_weights] * lax.axis_size('fsdp')), 'fsdp'...]
  transfers between devices with their start and end apart: 3 -> 2, of which waited for: 3 -> 1; matrix products, arithmetic and copies ran while one was open for 3% -> 3% of each run, Pallas kernels for 0% -> 0%
where the time goes in v1:
time: 549 us
  waiting for transfers between devices  448 us (82%)
  blocking collectives  63.6 us (12%)
  between operations  15.5 us (3%)
  matrix products  11.1 us (2%)
  other arithmetic  8.36 us (2%)
    psum x1, waiting for transfers between devices, per_device(): summed = lax.psum(outer_grad, 'rep')  448 us
    all_to_all x1, blocking collectives, per_device(): lax.all_to_all(jnp.stack([start_weights] * lax.axis_size('fsdp')), 'fsdp'...  63.6 us
  transfers between devices with their start and end apart: 2, of which 1 were waited for; matrix products, arithmetic and copies ran while one was open for 3% of the time, Pallas kernels for 0%

profile of v1, /device:TPU:1, one launch (start us, length us, event | category | flops | bytes accessed | tf_op | source)
XLA Modules:
  0.0 548.5 jit_solution(2103154530782895190)
XLA Ops:
  8.0 0.0 copy-start
  8.0 0.0 all-reduce.2.cloned.1.call-start
  8.1 2.8 convert_subtract_fusion
  10.8 0.0 all-reduce.2.cloned.1.call-update
  10.9 0.0 reduce-scatter.2.cloned.1.call-start
  10.9 0.0 copy-done
  10.9 8.2 %fusion.2 = f32[5120,512]{1,0:T(8,128)} fusion(bf16[512,5120]{1,0:T(8,128)(2,1)} %param.8, bf16[512,512]{1,0:T(8,128)(2,1)S(1)} %copy-done), kind=kOutput, calls=%fused_computation.7 | convolution fusion | flops 2684354560 | bytes 16252928 | tf_op jit(solution)/shard_map/dot_general | solution.py:28
  19.1 0.0 copy-start.1
  19.1 0.0 copy-start.2
  19.1 0.0 reduce-scatter.2.cloned.1.call-update
  19.1 448.4 %all-reduce.2.cloned.1.call-done = f32[640,512]{1,0:T(8,128)} async-done(((f32[640,512]{1,0:T(8,128)}), f32[640,512]{1,0:T(8,128)}) %all-reduce.2.cloned.1.call-update) | async-done | bytes 1310736 | tf_op jit(solution)/shard_map/psum | solution.py:13
  467.5 0.0 copy-done.1
  467.5 0.0 copy-done.2
  467.5 3.3 fusion.1
  470.8 0.0 slice-start
  470.8 0.4 stack.2
  471.3 0.0 slice-start.1
  471.3 63.6 %all_to_all.5 = bf16[8,640,512]{2,1,0:T(8,128)(2,1)S(1)} all-to-all(bf16[8,640,512]{2,1,0:T(8,128)(2,1)S(1)} %stack.2), channel_id=1, replica_groups=mesh['rep'=32,'fsdp'=8] {'fsdp'}, dimensions={0} | all-to-all | bytes 10485760 | tf_op jit(solution)/shard_map/all_to_all | solution.py:22
  534.9 0.0 slice-done
  534.9 0.0 slice-done.1
  534.9 2.9 fusion
  537.8 1.0 copy.9
  538.8 0.0 reduce-scatter.2.cloned.1.call-done
  538.8 2.2 convert_bitcast_fusion
  (1 shorter events, 0.0 us)
Async XLA Ops:
  8.0 2.9 copy-start
  8.0 459.5 %all-reduce.2.cloned.1.call-start = ((), (), s32[]{:S(2)}) async-start(), calls=%async_computation.2 | async-start | bytes 2621440 | tf_op jit(solution)/shard_map/psum | solution.py:13
  10.9 528.0 %reduce-scatter.2.cloned.1.call-start = ((), (), s32[]{:S(2)}) async-start(), calls=%async_computation.3 | async-start | bytes 11796480 | tf_op jit(solution)/shard_map/reduce_scatter | solution.py:27
  19.1 448.4 %copy-start.1 = (f32[640,512]{1,0:T(8,128)S(1)}, f32[640,512]{1,0:T(8,128)}, u32[]{:S(2)}) copy-start(f32[640,512]{1,0:T(8,128)} %param.6) | copy-start | bytes 3932164
  19.1 448.4 %copy-start.2 = (f32[640,512]{1,0:T(8,128)S(1)}, f32[640,512]{1,0:T(8,128)}, u32[]{:S(2)}) copy-start(f32[640,512]{1,0:T(8,128)} %param.7) | copy-start | bytes 3932164
  470.8 64.1 %slice-start = ((s8[5242880]{0:T(1024)(128)(4,1)}), s8[4194304]{0:T(1024)(128)(4,1)S(1)}, s32[]{:S(2)}) async-start(s8[5242880]{0:T(1024)(128)(4,1)} %bitcast.12), calls=%async_computation.4 | async-start | bytes 8388608
  471.3 63.6 %slice-start.1 = ((s8[5242880]{0:T(1024)(128)(4,1)}), s8[1048576]{0:T(1024)(128)(4,1)S(1)}, s32[]{:S(2)}) async-start(s8[5242880]{0:T(1024)(128)(4,1)} %bitcast.12), calls=%async_computation.5 | async-start | bytes 2097152
Sparse Core Ops, SparseCore 0:
  12.0 455.4 all-reduce.1
Sparse Core Ops, SparseCore 1:
  19.2 217.1 reduce-scatter.1

commit v2 on v0

--- a/solution.py
+++ b/solution.py
@@ -10,7 +10,7 @@
 def per_device(local_weights, global_weights, momentum, tokens, key_grad):
     replicas = lax.axis_size("rep")
     outer_grad = global_weights - local_weights[0].astype(jnp.float32)
-    summed = lax.psum(outer_grad, "rep")
+    summed = jnp.sum(lax.all_gather(outer_grad, "rep"), axis=0)
     average = summed / replicas
     new_momentum = momentum_rate * momentum + average
     new_global = global_weights - outer_rate * (average + momentum_rate * new_momentum)

time: 642 us -> 572 us (0.89)
  waiting for transfers between devices: 603 us -> 516 us
  other arithmetic: 8.64 us -> 23.9 us
    all_gather x0 -> x1, waiting for transfers between devices: none -> 378 us  [per_device(): summed = jnp.sum(lax.all_gather(outer_grad, 'rep'), axis=0)]
    psum x1 -> x0, waiting for transfers between devices: 293 us -> none  [per_device(): summed = lax.psum(outer_grad, 'rep')]
    reduce_scatter x1, waiting for transfers between devices: 207 us -> 25.4 us  [per_device(): lax.psum_scatter(lax.dot_general(columns, key_grad, (((0,), (0,)), ((), (...]
    reduce_sum x0 -> x1, other arithmetic: none -> 15.3 us  [per_device(): summed = jnp.sum(lax.all_gather(outer_grad, 'rep'), axis=0)]
    all_gather x1, waiting for transfers between devices: 103 us -> 112 us  [per_device(): lax.all_gather(start_weights, 'fsdp', axis=0, tiled=True)]
  transfers between devices with their start and end apart: 3 -> 3, of which waited for: 3 -> 3; matrix products, arithmetic and copies ran while one was open for 3% -> 5% of each run, Pallas kernels for 0% -> 0%
where the time goes in v2:
time: 572 us
  waiting for transfers between devices  516 us (90%)
  other arithmetic  23.9 us (4%)
  between operations  15.5 us (3%)
  matrix products  15 us (3%)
    all_gather x1, waiting for transfers between devices, per_device(): summed = jnp.sum(lax.all_gather(outer_grad, 'rep'), axis=0)  378 us
    all_gather x1, waiting for transfers between devices, per_device(): lax.all_gather(start_weights, 'fsdp', axis=0, tiled=True)  112 us
    reduce_scatter x1, waiting for transfers between devices, per_device(): lax.psum_scatter(lax.dot_general(columns, key_grad, (((0,), (0,)), ((), (...  25.4 us
    reduce_sum x1, other arithmetic, per_device(): summed = jnp.sum(lax.all_gather(outer_grad, 'rep'), axis=0)  15.3 us
  transfers between devices with their start and end apart: 3, of which 3 were waited for; matrix products, arithmetic and copies ran while one was open for 5% of the time, Pallas kernels for 0%

profile of v2, /device:TPU:1, one launch (start us, length us, event | category | flops | bytes accessed | tf_op | source)
XLA Modules:
  0.0 571.6 jit_solution(819586810412710003)
XLA Ops:
  8.0 0.0 copy-start
  8.0 0.0 all-gather.6.cloned.1.call-start
  8.1 2.8 convert_subtract_fusion
  10.8 0.0 all-gather.6.cloned.1.call-update
  10.9 0.0 reduce-scatter.2.cloned.1.call-start
  10.9 0.0 copy-done
  10.9 8.0 %fusion.2 = f32[5120,512]{1,0:T(8,128)} fusion(bf16[512,5120]{1,0:T(8,128)(2,1)} %param.8, bf16[512,512]{1,0:T(8,128)(2,1)S(1)} %copy-done), kind=kOutput, calls=%fused_computation.7 | convolution fusion | flops 2684354560 | bytes 16252928 | tf_op jit(solution)/shard_map/dot_general | solution.py:26
  18.9 0.0 reduce-scatter.2.cloned.1.call-update
  18.9 0.0 all-gather.4.cloned.1.call-start
  19.0 378.2 %all-gather.6.cloned.1.call-done = f32[20480,512]{1,0:T(8,128)} async-done(((f32[640,512]{1,0:T(8,128)}), f32[20480,512]{1,0:T(8,128)}) %all-gather.6.cloned.1.call-update) | async-done | bytes 41943056 | tf_op jit(solution)/shard_map/all_gather | solution.py:13
  397.2 0.0 copy-start.2
  397.2 15.3 %reduce_sum.9 = f32[640,512]{1,0:T(8,128)S(1)} reduce(f32[32,640,512]{2,1,0:T(8,128)} %bitcast.12, f32[]{:T(128)} %constant.1.clone.1), dimensions={0}, to_apply=%region_0.0 | reduce | flops 10158080 | bytes 43253764 | tf_op jit(solution)/shard_map/reduce_sum | solution.py:13
  412.5 0.0 copy-done.2
  412.5 3.6 fusion.1
  416.1 0.0 all-gather.4.cloned.1.call-update
  416.1 25.4 %reduce-scatter.2.cloned.1.call-done = f32[640,512]{1,0:T(8,128)} async-done(((f32[5120,512]{1,0:T(8,128)}), f32[640,512]{1,0:T(8,128)}) %reduce-scatter.2.cloned.1.call-update) | async-done | bytes 1310736 | tf_op jit(solution)/shard_map/reduce_scatter | solution.py:25
  441.5 2.2 convert_bitcast_fusion
  443.8 112.3 %all-gather.4.cloned.1.call-done = bf16[5120,512]{1,0:T(8,128)(2,1)} async-done(((bf16[640,512]{1,0:T(8,128)(2,1)}), bf16[5120,512]{1,0:T(8,128)(2,1)}) %all-gather.4.cloned.1.call-update) | async-done | bytes 5242896 | tf_op jit(solution)/shard_map/all_gather | solution.py:21
  556.1 0.0 copy-start.1
  556.1 7.0 %fusion = bf16[512,512]{0,1:T(8,128)(2,1)S(1)} fusion(bf16[5120,512]{1,0:T(8,128)(2,1)} %all-gather.4.cloned.1.call-done, bf16[512,5120]{1,0:T(8,128)(2,1)} %param.8), kind=kOutput, calls=%fused_computation.4 | convolution fusion | flops 2684616704 | bytes 11010048 | tf_op jit(solution)/shard_map/dot_general | solution.py:19
  563.1 1.0 copy.9
  564.2 0.0 copy-done.1
Async XLA Ops:
  8.0 2.9 copy-start
  8.0 389.2 %all-gather.6.cloned.1.call-start = ((), (), s32[]{:S(2)}) async-start(), calls=%async_computation.3 | async-start | bytes 43253760 | tf_op jit(solution)/shard_map/all_gather | solution.py:13
  10.9 430.7 %reduce-scatter.2.cloned.1.call-start = ((), (), s32[]{:S(2)}) async-start(), calls=%async_computation.2 | async-start | bytes 11796480 | tf_op jit(solution)/shard_map/reduce_scatter | solution.py:25
  18.9 537.2 %all-gather.4.cloned.1.call-start = ((), (), s32[]{:S(2)}) async-start(), calls=%async_computation.1 | async-start | bytes 5898240 | tf_op jit(solution)/shard_map/all_gather | solution.py:21
  397.2 15.3 %copy-start.2 = (f32[640,512]{1,0:T(8,128)S(1)}, f32[640,512]{1,0:T(8,128)}, u32[]{:S(2)}) copy-start(f32[640,512]{1,0:T(8,128)} %param.6) | copy-start | bytes 3932164
  556.1 8.0 %copy-start.1 = (bf16[512,512]{1,0:T(8,128)(2,1)S(1)}, bf16[512,512]{1,0:T(8,128)(2,1)}, u32[]{:S(2)}) copy-start(bf16[512,512]{1,0:T(8,128)(2,1)} %param.9) | copy-start | bytes 1572868
Sparse Core Ops, SparseCore 0:
  12.0 385.1 all-gather.5
Sparse Core Ops, SparseCore 1:
  19.0 422.5 reduce-scatter.1
  443.2 112.9 all-gather.3
